TPU v7x, 256 devices: a whole 4x4x8 slice. The times are simulated.
256 devices in a mesh: lat: 64 (over x, z, core), lev: 4 (over y).
Axes of the slice: x: 4, y: 4, z: 8, core: 2. Of those that a mesh axis runs over, the one named last changes fastest.
Arguments:
- fine_field: bfloat16 [2, 1280, 32, 1280], P(None, 'lat', 'lev'), may hold values from -6 to 6
- fwd_table: bfloat16 [320, 641, 1280], P('lat'), may hold values from -0.125 to 0.125
- inv_table: bfloat16 [320, 641, 640], P('lat'), may hold values from -0.25 to 0.25
- pair_order: int32 [320], replicated, may hold values from 0 to 319, each once
Outputs:
- coarse: bfloat16 [2, 640, 32, 1280], P(None, 'lat', 'lev')
Inputs may be any that keep to these rules, and one draw needn't show every extreme that they name: Each value appears once; slot s holds the wavenumbers pair_order[s] and 639 - pair_order[s].
All inputs are finite; a program needn't handle non-finite values.
Results may differ from a plain program's by a relative error of at most 0.0059.
Values may be sent and summed in bfloat16 or wider, within the bound.
A program may use at most 128 MiB of HBM per device.

v0:
```python
import jax
import jax.numpy as jnp
from jax import lax
from jax.sharding import PartitionSpec as P


def carried_mask(row_start, row_count, wave_ids):
    row_ids = row_start + jnp.arange(row_count, dtype=jnp.int32)
    return 2 * wave_ids[None, :] < 20 + 4 * row_ids[:, None]


def slot_groups(pair_ids, total_waves, table_rows):
    row_ids = jnp.arange(table_rows, dtype=jnp.int32)
    boundary = total_waves - pair_ids[:, None]
    second = row_ids[None, :] >= boundary
    offset = jnp.where(second, row_ids[None, :] - boundary, row_ids[None, :])
    return 2 * second.astype(jnp.int32) + offset % 2


def forward_rows(slot_tables, incoming, groups):
    level_count = incoming.shape[2]
    local_slots = incoming.shape[5]
    table_rows = slot_tables.shape[1]
    product = jnp.einsum(
        "srl,plxcws->srwpxc", slot_tables, incoming, preferred_element_type=jnp.float32
    )
    product = product.reshape(local_slots, table_rows, 4, level_count * 2)
    return jnp.take_along_axis(product, groups[:, :, None, None], axis=2)[:, :, 0, :]


def inverse_rows(back_tables, spectra, groups, my_pairs, total_waves):
    local_slots = back_tables.shape[0]
    row_count = back_tables.shape[2]
    level_count = spectra.shape[2] // 2
    chosen = groups[:, :, None] == jnp.arange(4, dtype=jnp.int32)[None, None, :]
    spread = jnp.where(chosen[:, :, :, None], spectra[:, :, None, :], jnp.zeros((), jnp.bfloat16))
    summed = jnp.einsum("srj,srgx->gxsj", back_tables, spread, preferred_element_type=jnp.float32)
    summed = summed.reshape(2, 2, level_count, 2, local_slots, row_count)
    halves = jnp.stack([summed[:, 0] + summed[:, 1], summed[:, 0] - summed[:, 1]], axis=1)
    pair_waves = jnp.stack([my_pairs, total_waves - 1 - my_pairs])
    coarse_ids = jnp.arange(row_count, dtype=jnp.int32)
    keep_coarse = 2 * pair_waves[:, :, None] < 20 + 4 * coarse_ids[None, None, :]
    kept = jnp.where(keep_coarse[:, None, None, None, :, :], halves, jnp.zeros((), jnp.float32))
    return kept.astype(jnp.bfloat16)


def on_device(fine_field, fwd_table, inv_table, pair_order):
    hemispheres, lat_band, level_count, columns = fine_field.shape
    total_waves = columns // 2
    slot_count = pair_order.shape[0]
    local_slots = fwd_table.shape[0]
    table_rows = fwd_table.shape[1]
    lat_place = lax.axis_index("lat")
    wave_ids = jnp.arange(total_waves, dtype=jnp.int32)
    keep_fine = carried_mask(lat_place * lat_band, lat_band, wave_ids)
    values = fine_field.astype(jnp.float32).reshape(
        hemispheres, lat_band, level_count, 2, total_waves
    )
    values = jnp.where(keep_fine[None, :, None, None, :], values, jnp.zeros((), jnp.float32))
    even_part = (values[0] + values[1]).astype(jnp.bfloat16)
    odd_part = (values[0] - values[1]).astype(jnp.bfloat16)
    folded = jnp.stack([even_part, odd_part])
    slot_waves = jnp.concatenate([pair_order, total_waves - 1 - pair_order])
    selector = (wave_ids[:, None] == slot_waves[None, :]).astype(jnp.bfloat16)
    picked = jnp.einsum("plxcm,mk->plxck", folded, selector, preferred_element_type=jnp.float32)
    outgoing = picked.astype(jnp.bfloat16).reshape(2, lat_band, level_count, 2, 2, slot_count)
    my_pairs = lax.dynamic_slice_in_dim(pair_order, lat_place * local_slots, local_slots)
    groups = slot_groups(my_pairs, total_waves, table_rows)
    incoming = lax.all_to_all(outgoing, "lat", split_axis=5, concat_axis=1, tiled=True)
    spectra = forward_rows(fwd_table, incoming, groups).astype(jnp.bfloat16)
    shaped = inverse_rows(inv_table, spectra, groups, my_pairs, total_waves)
    arrived = lax.all_to_all(shaped, "lat", split_axis=5, concat_axis=4, tiled=True)
    coarse_band = arrived.shape[5]
    back_selector = jnp.transpose(selector).reshape(2, slot_count, total_waves)
    placed = jnp.einsum(
        "whxcsj,wsm->hjxcm", arrived, back_selector, preferred_element_type=jnp.float32
    )
    return placed.astype(jnp.bfloat16).reshape(hemispheres, coarse_band, level_count, columns)


def solution(mesh):
    return jax.shard_map(
        on_device,
        mesh=mesh,
        in_specs=(P(None, "lat", "lev", None), P("lat", None, None), P("lat", None, None), P()),
        out_specs=P(None, "lat", "lev", None),
        check_vma=False,
    )
```

profile of v0, /device:TPU:1, one launch (start us, length us, event | category | flops | bytes accessed | tf_op | source)
XLA Modules:
  0.0 239.6 jit_solution(3572566524015139678)
XLA Ops:
  0.0 0.7 broadcast_subtract_fusion
  0.7 0.8 pad_add_fusion
  1.5 0.1 broadcast_compare_fusion
  1.5 1.3 convert_select_fusion
  2.8 0.1 add_convert_fusion
  3.0 0.9 fusion.16
  3.9 0.8 reshape.313
  4.7 8.4 %copy.52 = bf16[2,20,8,2,2,320]{1,2,4,3,0,5:T(8,128)(2,1)} copy(bf16[2,20,8,2,2,320]{5,4,2,3,1,0:T(2,128)(2,1)S(1)} %reshape.313) | data formatting | bytes 1638400 | tf_op jit(solution)/shard_map/reshape | solution.py:66
  13.1 12.4 %reshape.335 = bf16[64,2,3200]{2,1,0:T(2,128)(2,1)} reshape(bf16[320,2,2,2,8,20]{5,4,3,2,1,0:T(8,128)(2,1)} %bitcast.86) | data formatting | bytes 1638400
  25.5 13.0 %all-to-all-start = ((bf16[64,2,3200]{2,1,0:T(2,128)(2,1)}), bf16[64,2,3200]{2,1,0:T(2,128)(2,1)S(1)}, u32[]{:S(2)}, u32[]{:S(2)}) async-start(bf16[64,2,3200]{2,1,0:T(2,128)(2,1)} %reshape.335), calls=%async_computation | async-start | bytes 1638400 | tf_op jit(solution)/shard_map/all_to_all | solution.py:69
  38.5 0.8 dynamic-slice_bitcast_fusion
  39.3 0.1 compare_select_fusion
  39.4 0.1 reshape.321
  39.5 0.1 compare_and_fusion
  39.6 0.1 broadcast_compare_fusion.1
  39.7 0.1 fusion.47
  39.8 22.3 %all-to-all-done = bf16[64,2,3200]{2,1,0:T(2,128)(2,1)S(1)} async-done(((bf16[64,2,3200]{2,1,0:T(2,128)(2,1)}), bf16[64,2,3200]{2,1,0:T(2,128)(2,1)S(1)}, u32[]{:S(2)}, u32[]{:S(2)}) %all-to-all-start) | async-done | bytes 819232 | tf_op jit(solution)/shard_map/all_to_all | solution.py:69
  62.1 14.5 %reshape.336 = bf16[320,2,2,2,8,20]{5,4,3,2,1,0:T(8,128)(2,1)} reshape(bf16[64,2,3200]{2,1,0:T(2,128)(2,1)S(1)} %all-to-all-done) | data formatting | bytes 1638400
  76.6 10.9 %copy.73 = bf16[2,64,20,8,2,2,5]{2,1,3,5,4,0,6:T(8,128)(2,1)} copy(bf16[2,64,20,8,2,2,5]{2,3,5,4,0,6,1:T(8,128)(2,1)} %bitcast.87) | data formatting | bytes 1638400 | tf_op jit(solution)/shard_map/all_to_all | solution.py:69
  87.5 10.1 %reshape.334 = bf16[2,1280,8,2,2,5]{1,2,4,3,0,5:T(8,128)(2,1)S(1)} reshape(bf16[2,64,20,8,2,2,5]{2,1,3,5,4,0,6:T(8,128)(2,1)} %copy.73) | data formatting | bytes 1638400 | tf_op jit(solution)/shard_map/all_to_all | solution.py:69
  97.6 5.9 %fusion.19 = bf16[5,641,2,2,8,2]{1,4,2,5,3,0:T(8,128)(2,1)S(1)} fusion(bf16[2,1280,8,2,2,5]{1,2,4,3,0,5:T(8,128)(2,1)S(1)} %reshape.334, bf16[5,641,1280]{2,1,0:T(8,128)(2,1)} %param.5), kind=kOutput, calls=%fused_computation.15 | convolution fusion | flops 525107200 | bytes 9434240 | tf_op jit(solution)/shard_map/srl,plxcws->srwpxc/dot_general | solution.py:24
  103.4 0.4 copy.56
  103.9 1.2 reshape.314
  105.0 3.9 %copy.57 = bf16[5,641,4,16]{3,2,1,0:T(4,128)(2,1)S(1)} copy(bf16[5,641,4,16]{1,3,2,0:T(8,128)(2,1)} %reshape.314) | data formatting | bytes 820480 | tf_op jit(solution)/shard_map/reshape | solution.py:27
  108.9 43.0 %gather_fusion = bf16[3205,16]{1,0:T(8,128)(2,1)} fusion(bf16[5,641,4,16]{3,2,1,0:T(4,128)(2,1)S(1)} %copy.57, s32[3205]{0:T(1024)S(1)} %reshape.321), kind=kCustom, calls=%fused_computation | custom fusion | bytes 243580 | tf_op jit(solution)/shard_map/jit(take_along_axis)/gather | solution.py:28
  151.9 1.4 copy.58
  153.3 0.2 gather.7
  153.6 3.0 %fusion.27 = f32[4,16,5,640]{3,1,0,2:T(8,128)S(1)} fusion(bf16[5,641,640]{2,1,0:T(8,128)(2,1)} %param.6, pred[5,641,4]{1,2,0:T(4,128)(4,1)S(1)} %iota_compare_fusion.2, bf16[5,641,16]{1,2,0:T(8,128)(2,1)S(1)} %fusion.43), kind=kOutput, calls=%fused_computation.17 | convolution fusion | flops 262758720 | bytes 5036980 | tf_op jit(solution)/shard_map/srj,srgx->gxsj/dot_general | solution.py:37
  156.6 0.5 reshape.315
  157.1 0.3 fusion.57
  157.4 0.1 copy_add_fusion
  157.5 0.1 fusion.38
  157.6 9.9 %copy.62 = bf16[2,2,8,2,5,640]{2,3,4,1,0,5:T(2,128)(2,1)} copy(bf16[2,2,8,2,5,640]{5,2,4,3,1,0:T(8,128)(2,1)S(1)} %fusion.38) | data formatting | bytes 819200 | tf_op jit(solution)/shard_map/convert_element_type | solution.py:44
  167.5 18.5 %reshape.337 = bf16[64,2,1600]{2,1,0:T(2,128)(2,1)} reshape(bf16[640,2,2,5,2,8]{5,4,3,2,1,0:T(2,128)(2,1)} %bitcast.84) | data formatting | bytes 819200
  186.0 6.2 %all-to-all-start.1 = ((bf16[64,2,1600]{2,1,0:T(2,128)(2,1)}), bf16[64,2,1600]{2,1,0:T(2,128)(2,1)S(1)}, u32[]{:S(2)}, u32[]{:S(2)}) async-start(bf16[64,2,1600]{2,1,0:T(2,128)(2,1)} %reshape.337), calls=%async_computation.1 | async-start | bytes 851968 | tf_op jit(solution)/shard_map/all_to_all | solution.py:72
  192.2 0.1 eq.43
  192.3 15.2 %all-to-all-done.1 = bf16[64,2,1600]{2,1,0:T(2,128)(2,1)S(1)} async-done(((bf16[64,2,1600]{2,1,0:T(2,128)(2,1)}), bf16[64,2,1600]{2,1,0:T(2,128)(2,1)S(1)}, u32[]{:S(2)}, u32[]{:S(2)}) %all-to-all-start.1) | async-done | bytes 409632 | tf_op jit(solution)/shard_map/all_to_all | solution.py:72
  207.5 5.7 %reshape.338 = bf16[640,2,2,5,2,8]{5,4,3,2,1,0:T(2,128)(2,1)} reshape(bf16[64,2,1600]{2,1,0:T(2,128)(2,1)S(1)} %all-to-all-done.1) | data formatting | bytes 819200
  213.3 20.6 %copy.75 = bf16[2,2,8,2,5,64,10]{6,2,4,5,3,1,0:T(8,128)(2,1)} copy(bf16[2,2,8,2,5,64,10]{2,3,4,1,0,6,5:T(2,128)(2,1)} %bitcast.85) | data formatting | bytes 819200 | tf_op jit(solution)/shard_map/all_to_all | solution.py:72
  233.9 4.3 %fusion.30 = bf16[2,10,8,2,640]{4,1,3,2,0:T(8,128)(2,1)S(1)} fusion(bf16[2,2,8,2,320,10]{5,2,4,3,1,0:T(8,128)(2,1)} %bitcast.88, s32[2,320]{1,0:T(2,128)S(1)} %eq.43), kind=kOutput, calls=%fused_computation.18 | convolution fusion | flops 262758400 | bytes 821760 | tf_op jit(solution)/shard_map/whxcsj,wsm->hjxcm/dot_general | solution.py:75
  238.2 0.3 copy.66
  238.5 1.0 reshape.316
  (10 shorter events, 0.1 us)
Async XLA Ops:
  25.5 36.6 %all-to-all-start = ((bf16[64,2,3200]{2,1,0:T(2,128)(2,1)}), bf16[64,2,3200]{2,1,0:T(2,128)(2,1)S(1)}, u32[]{:S(2)}, u32[]{:S(2)}) async-start(bf16[64,2,3200]{2,1,0:T(2,128)(2,1)} %reshape.335), calls=%async_computation | async-start | bytes 1638400 | tf_op jit(solution)/shard_map/all_to_all | solution.py:69
  186.0 21.5 %all-to-all-start.1 = ((bf16[64,2,1600]{2,1,0:T(2,128)(2,1)}), bf16[64,2,1600]{2,1,0:T(2,128)(2,1)S(1)}, u32[]{:S(2)}, u32[]{:S(2)}) async-start(bf16[64,2,1600]{2,1,0:T(2,128)(2,1)} %reshape.337), calls=%async_computation.1 | async-start | bytes 851968 | tf_op jit(solution)/shard_map/all_to_all | solution.py:72
where the time goes:
time: 241 us; the launch traced here: 240 us
  local copies, waits for them, and re-layouts  164 us (68%)
  waiting for transfers between devices  37.5 us (16%)
  starting transfers between devices  19.2 us (8%)
  matrix products  14.1 us (6%)
  other arithmetic  4.33 us (2%)
    unnamed x6, local copies, waits for them, and re-layouts  51.1 us
    gather x4, local copies, waits for them, and re-layouts, forward_rows(): jnp.take_along_axis(product, groups[:, :, None, None], axis=2)[:, :, 0, :]  44.7 us
    all_to_all x1, waiting for transfers between devices, on_device(): lax.all_to_all(outgoing, 'lat', split_axis=5, concat_axis=1, tiled=True)  22.3 us
    all_to_all x2, local copies, waits for them, and re-layouts, on_device(): lax.all_to_all(outgoing, 'lat', split_axis=5, concat_axis=1, tiled=True)  21 us
    all_to_all x1, local copies, waits for them, and re-layouts, on_device(): lax.all_to_all(shaped, 'lat', split_axis=5, concat_axis=4, tiled=True)  20.6 us
    all_to_all x1, waiting for transfers between devices, on_device(): lax.all_to_all(shaped, 'lat', split_axis=5, concat_axis=4, tiled=True)  15.2 us
    all_to_all x1, starting transfers between devices, on_device(): lax.all_to_all(outgoing, 'lat', split_axis=5, concat_axis=1, tiled=True)  13 us
    convert_element_type x1, local copies, waits for them, and re-layouts, inverse_rows(): return kept.astype(jnp.bfloat16)  9.91 us
  transfers between devices with their start and end apart: 2, of which 2 were waited for; matrix products, arithmetic and copies ran while one was open for 1% of the time, Pallas kernels for 0%

commit v1 on v0

v1 whole, which is shorter than its diff:
```python
import jax
import jax.numpy as jnp
from jax import lax
from jax.experimental import pallas as pl
from jax.experimental.pallas import tpu as pltpu
from jax.sharding import PartitionSpec as P

MESH = pl.DeviceIdType.MESH
WAVES = 640
FINE = 1280
COARSE = 640
BANDS = 64
BAND = FINE // BANDS
CBAND = COARSE // BANDS
SLOTS = 5
ROWS = 641
BF = jnp.bfloat16
F32 = jnp.float32


def lanes(shape):
    return lax.broadcasted_iota(jnp.int32, shape, len(shape) - 1)


def block_transpose(a):
    lane = lanes(a[0].shape)
    low = lane < 64
    even = (lane // 32) % 2 == 0
    c0 = jnp.where(low, a[0], pltpu.roll(a[2], 64, 1))
    c2 = jnp.where(low, pltpu.roll(a[0], 64, 1), a[2])
    c1 = jnp.where(low, a[1], pltpu.roll(a[3], 64, 1))
    c3 = jnp.where(low, pltpu.roll(a[1], 64, 1), a[3])
    b0 = jnp.where(even, c0, pltpu.roll(c1, 32, 1))
    b1 = jnp.where(even, pltpu.roll(c0, 96, 1), c1)
    b2 = jnp.where(even, c2, pltpu.roll(c3, 32, 1))
    b3 = jnp.where(even, pltpu.roll(c2, 96, 1), c3)
    return b0, b1, b2, b3


def half_swap(a, b):
    low = lanes(a.shape) < 64
    return (
        jnp.where(low, a, pltpu.roll(b, 64, 1)),
        jnp.where(low, pltpu.roll(a, 64, 1), b),
    )


def kernel(
    pair_ref, wave_ref, fine_ref, fwd_hbm, inv_hbm, out_ref,
    fwd, inv, folded, sel, wide, narrow, acc,
    send_ab, send_c, recv_ab, recv_c, back_ab, back_c, home_ab, home_c,
    fwd_sem, inv_sem, out_sem1, in_sem1, out_sem2, in_sem2,
):
    me = lax.axis_index("lat")
    lev = lax.axis_index("lev")
    barrier = pltpu.get_barrier_semaphore()

    @pl.loop(1, BANDS)
    def _(t):
        pl.semaphore_signal(
            barrier, inc=1, device_id=(lax.rem(me + t, BANDS), lev), device_id_type=MESH
        )

    for s in range(SLOTS):
        pltpu.make_async_copy(fwd_hbm.at[s], fwd.at[s], fwd_sem.at[s]).start()
        pltpu.make_async_copy(inv_hbm.at[s], inv.at[s], inv_sem.at[s]).start()

    @pl.loop(0, BAND)
    def _(i):
        north = fine_ref[0, i].astype(F32)
        south = fine_ref[1, i].astype(F32)
        m = lanes((8, 2 * WAVES))
        m = jnp.where(m >= WAVES, m - WAVES, m)
        kept = 2 * m < 20 + 4 * (me * BAND + i)
        even = jnp.where(kept, north + south, 0.0)
        odd = jnp.where(kept, north - south, 0.0)
        rows = jnp.concatenate(
            [even[:, :WAVES], even[:, WAVES:], odd[:, :WAVES], odd[:, WAVES:]], axis=0
        )
        folded[pl.ds(pl.multiple_of(i * 32, 32), 32), :] = rows.astype(BF)

    sel[...] = jnp.where(
        wave_ref[...] == lanes((WAVES, WAVES)), 1.0, 0.0
    ).astype(BF)

    def pick(first, count):
        return lax.dot_general(
            sel[first : first + count, :], folded[...], (((1,), (1,)), ((), ())),
            preferred_element_type=F32,
        )

    def exchange(src, dst, out_sem, in_sem):
        pltpu.make_async_copy(src.at[me], dst.at[me], in_sem).start()

        @pl.loop(1, BANDS)
        def _(t):
            to = lax.rem(me + t, BANDS)
            pltpu.make_async_remote_copy(
                src_ref=src.at[to], dst_ref=dst.at[me], send_sem=out_sem, recv_sem=in_sem,
                device_id=(to, lev), device_id_type=MESH,
            ).start()

    def arrive(dst, in_sem):
        pltpu.make_async_copy(dst, dst, in_sem).wait()

    def left(src, out_sem):
        part = src.at[pl.ds(0, BANDS - 1)]
        pltpu.make_async_copy(part, part, out_sem).wait()

    for ch in range(2):
        g = pick(256 * ch, 256)
        for q in range(BAND // 4):
            cols = g[:, 128 * q : 128 * (q + 1)]
            parts = block_transpose([cols[64 * k : 64 * (k + 1)] for k in range(4)])
            for k in range(4):
                wide[pl.ds(4 * q + k, BANDS, stride=BAND), :] = parts[k]
        send_ab.at[ch].reshape(FINE, 128)[...] = wide[...].astype(BF)
        if ch == 0:
            pl.semaphore_wait(barrier, BANDS - 1)
        exchange(send_ab.at[ch], recv_ab.at[ch], out_sem1.at[ch], in_sem1.at[ch])

    g = pick(512, 128)
    for q in range(BAND // 4):
        cols = g[:, 128 * q : 128 * (q + 1)]
        parts = half_swap(cols[:64], cols[64:])
        for k in range(2):
            wide[pl.ds(2 * q + k, BANDS, stride=BAND // 2), :] = parts[k]
    send_c.reshape(FINE // 2, 128)[...] = wide[: FINE // 2].astype(BF)
    exchange(send_c, recv_c, out_sem1.at[2], in_sem1.at[2])

    row = lax.broadcasted_iota(jnp.int32, (ROWS, 128), 0)
    lane = lanes((ROWS, 128))

    def transform(slot, x, fold_lanes, owned):
        pltpu.make_async_copy(fwd_hbm.at[slot], fwd.at[slot], fwd_sem.at[slot]).wait()
        product = jnp.dot(fwd[slot], x, preferred_element_type=F32)
        product = fold_lanes(product)
        boundary = WAVES - pair_ref[me * SLOTS + slot]
        second = row >= boundary
        parity = jnp.where(second, row - boundary, row) % 2
        wave = second.astype(jnp.int32)
        keep = owned(lane, wave) & ((lane // 16) % 2 == parity)
        spectra = jnp.where(keep, product, 0.0).astype(BF)
        pltpu.make_async_copy(inv_hbm.at[slot], inv.at[slot], inv_sem.at[slot]).wait()
        return lax.dot_general(
            inv[slot], spectra, (((0,), (0,)), ((), ())), preferred_element_type=F32
        )

    def hemispheres(v):
        first = (lanes(v.shape) // 16) % 2 == 0
        other = jnp.where(first, pltpu.roll(v, 112, 1), pltpu.roll(v, 16, 1))
        return other + jnp.where(first, v, -v)

    for ch in range(2):
        arrive(recv_ab.at[ch], in_sem1.at[ch])
        x = recv_ab.at[ch].reshape(FINE, 128)[...]
        v = 0.0
        for half in range(2):
            v += transform(
                2 * ch + half, x, lambda p: p,
                lambda lane, wave: lane // 32 == 2 * half + wave,
            )
        back_ab.at[ch].reshape(COARSE, 128)[...] = hemispheres(v).astype(BF)
        exchange(back_ab.at[ch], home_ab.at[ch], out_sem2.at[ch], in_sem2.at[ch])

    arrive(recv_c, in_sem1.at[2])
    x = recv_c.reshape(FINE // 2, 128)[...].astype(F32)
    upper = (lanes(x.shape) // 32) % 2 == 0
    wide[pl.ds(0, FINE // 2, stride=2), :] = jnp.where(upper, x, 0.0)
    wide[pl.ds(1, FINE // 2, stride=2), :] = jnp.where(upper, 0.0, x)
    v = transform(
        4, wide[...].astype(BF), lambda p: p + pltpu.roll(p, 96, 1),
        lambda lane, wave: lane // 32 == 2 * wave,
    )
    wide[:COARSE] = hemispheres(v)
    for k in range(CBAND // 2):
        a = wide[pl.ds(2 * k, BANDS, stride=CBAND), :]
        b = wide[pl.ds(2 * k + 1, BANDS, stride=CBAND), :]
        narrow[pl.ds(k, BANDS, stride=6), :] = jnp.where(
            (lanes(a.shape) // 32) % 2 == 0, a, pltpu.roll(b, 32, 1)
        )
    narrow[pl.ds(5, BANDS, stride=6), :] = jnp.zeros((BANDS, 128), F32)
    back_c.reshape(6 * BANDS, 128)[...] = narrow[...].astype(BF)
    exchange(back_c, home_c, out_sem2.at[2], in_sem2.at[2])

    def place(first, columns):
        count = columns.shape[0]
        return lax.dot_general(
            columns, sel[first : first + count, :], (((0,), (0,)), ((), ())),
            preferred_element_type=F32,
        )

    for ch in range(2):
        arrive(home_ab.at[ch], in_sem2.at[ch])
        wide[:COARSE] = home_ab.at[ch].reshape(COARSE, 128)[...].astype(F32)
        groups = []
        for q in range(3):
            js = [min(4 * q + k, CBAND - 1) for k in range(4)]
            groups.append(
                jnp.concatenate(
                    block_transpose([wide[pl.ds(j, BANDS, stride=CBAND), :] for j in js]), axis=0
                ).astype(BF)
            )
        placed = place(256 * ch, jnp.concatenate(groups, axis=1))
        if ch == 0:
            acc[...] = placed
        else:
            acc[...] += placed
    arrive(home_c, in_sem2.at[2])
    wide[: 6 * BANDS] = home_c.reshape(6 * BANDS, 128)[...].astype(F32)
    groups = []
    for q in range(3):
        parts = half_swap(*[wide[pl.ds(2 * q + k, BANDS, stride=6), :] for k in range(2)])
        groups.append(jnp.concatenate(parts, axis=0).astype(BF))
    acc[...] += place(512, jnp.concatenate(groups, axis=1))

    @pl.loop(0, CBAND)
    def _(j):
        rows = acc[pl.ds(pl.multiple_of(j * 32, 32), 32), :]
        kept = 2 * lanes(rows.shape) < 20 + 4 * (me * CBAND + j)
        rows = jnp.where(kept, rows, 0.0).astype(BF)
        for h in range(2):
            for c in range(2):
                at = 16 * h + 8 * c
                out_ref[h, j, :, c * WAVES : (c + 1) * WAVES] = rows[at : at + 8]

    for ch in range(2):
        left(send_ab.at[ch], out_sem1.at[ch])
        left(back_ab.at[ch], out_sem2.at[ch])
    left(send_c, out_sem1.at[2])
    left(back_c, out_sem2.at[2])


def on_device(fine_field, fwd_table, inv_table, pair_order):
    low = jnp.transpose(pair_order.reshape(BANDS, SLOTS))
    waves = jnp.stack([low, WAVES - 1 - low], axis=1).reshape(WAVES, 1)
    vmem = pl.BlockSpec(memory_space=pltpu.VMEM)
    hbm = pl.BlockSpec(memory_space=pl.ANY)
    ab1 = (2, BANDS, BAND // 2, 2, 128)
    c1 = (BANDS, BAND // 4, 2, 128)
    ab2 = (2, BANDS, CBAND // 2, 2, 128)
    c2 = (BANDS, 3, 2, 128)
    return pl.pallas_call(
        kernel,
        out_shape=jax.ShapeDtypeStruct((2, CBAND, 8, 2 * WAVES), BF),
        in_specs=[pl.BlockSpec(memory_space=pltpu.SMEM), vmem, vmem, hbm, hbm],
        out_specs=vmem,
        scratch_shapes=[
            pltpu.VMEM((SLOTS, ROWS, FINE), BF),
            pltpu.VMEM((SLOTS, ROWS, COARSE), BF),
            pltpu.VMEM((BAND * 32, WAVES), BF),
            pltpu.VMEM((WAVES, WAVES), BF),
            pltpu.VMEM((FINE, 128), F32),
            pltpu.VMEM((6 * BANDS, 128), F32),
            pltpu.VMEM((384, WAVES), F32),
            pltpu.VMEM(ab1, BF), pltpu.VMEM(c1, BF),
            pltpu.VMEM(ab1, BF), pltpu.VMEM(c1, BF),
            pltpu.VMEM(ab2, BF), pltpu.VMEM(c2, BF),
            pltpu.VMEM(ab2, BF), pltpu.VMEM(c2, BF),
            pltpu.SemaphoreType.DMA((SLOTS,)), pltpu.SemaphoreType.DMA((SLOTS,)),
            pltpu.SemaphoreType.DMA((3,)), pltpu.SemaphoreType.DMA((3,)),
            pltpu.SemaphoreType.DMA((3,)), pltpu.SemaphoreType.DMA((3,)),
        ],
        compiler_params=pltpu.CompilerParams(
            collective_id=0, has_side_effects=True, vmem_limit_bytes=48 << 20
        ),
    )(pair_order, waves, fine_field, fwd_table, inv_table)


def solution(mesh):
    return jax.shard_map(
        on_device,
        mesh=mesh,
        in_specs=(P(None, "lat", "lev", None), P("lat", None, None), P("lat", None, None), P()),
        out_specs=P(None, "lat", "lev", None),
        check_vma=False,
    )
```

time: 241 us -> 50.7 us (0.21)
  local copies, waits for them, and re-layouts: 164 us -> 5.99 us
  Pallas kernels: 0 us -> 44.4 us
  waiting for transfers between devices: 37.5 us -> 0 us
  starting transfers between devices: 19.2 us -> 0 us
  matrix products: 14.1 us -> 0 us
  other arithmetic: 4.33 us -> 0.03 us
    unnamed x6 -> x7, local copies, waits for them, and re-layouts: 51.1 us -> 4.75 us
    gather x4 -> x0, local copies, waits for them, and re-layouts: 44.7 us -> none  [forward_rows(): jnp.take_along_axis(product, groups[:, :, None, None], axis=2)[:, :, 0, :]]
    pallas_call x0 -> x1, Pallas kernels: none -> 44.4 us  [on_device(): pl.pallas_call(kernel, out_shape=jax.ShapeDtypeStruct((2, CBAND, 8, 2 * W...]
    all_to_all x3 -> x0, local copies, waits for them, and re-layouts: 41.6 us -> none  [the longest x2 21 us: on_device(): lax.all_to_all(outgoing, 'lat', split_axis=5, concat_axis=1, tiled=True)]
    all_to_all x2 -> x0, waiting for transfers between devices: 37.5 us -> none  [the longest x1 22.3 us: on_device(): lax.all_to_all(outgoing, 'lat', split_axis=5, concat_axis=1, tiled=True)]
    all_to_all x2 -> x0, starting transfers between devices: 19.2 us -> none  [the longest x1 13 us: on_device(): lax.all_to_all(outgoing, 'lat', split_axis=5, concat_axis=1, tiled=True)]
    reshape x6 -> x2, local copies, waits for them, and re-layouts: 15.7 us -> 1.08 us  [the longest x1 0.81 us: on_device(): low = jnp.transpose(pair_order.reshape(BANDS, SLOTS))]
    dot_general x4 -> x0, matrix products: 14.1 us -> none  [the longest x1 5.86 us: forward_rows(): jnp.einsum('srl,plxcws->srwpxc', slot_tables, incoming, preferred_element...]
  transfers between devices with their start and end apart: 2 -> 0, of which waited for: 2 -> 0; matrix products, arithmetic and copies ran while one was open for 1% -> 0% of each run, Pallas kernels for 0% -> 0%
where the time goes in v1:
time: 50.7 us; the launch traced here: 50.5 us
  Pallas kernels  44.4 us (88%)
  local copies, waits for them, and re-layouts  5.99 us (12%)
    pallas_call x1, Pallas kernels, on_device(): pl.pallas_call(kernel, out_shape=jax.ShapeDtypeStruct((2, CBAND, 8, 2 * W...  44.4 us
    unnamed x7, local copies, waits for them, and re-layouts  4.75 us

profile of v1, /device:TPU:1, one launch (start us, length us, event | category | flops | bytes accessed | tf_op | source)
XLA Modules:
  0.0 50.5 jit_solution(15421175443790948685)
XLA Ops:
  0.0 0.8 %reshape.6 = s32[64,5]{1,0:T(8,128)S(1)} reshape(s32[320]{0:T(512)} %pair_ref.1) | data formatting | bytes 2560 | tf_op jit(solution)/shard_map/reshape | solution.py:235
  0.8 0.1 copy.8
  0.9 0.1 copy.9
  1.0 0.3 reshape.8.wave_ref
  1.3 0.0 copy-start
  1.3 2.2 %copy-done = bf16[5,641,640]{2,1,0:T(8,128)(2,1)S(1)} copy-done((bf16[5,641,640]{2,1,0:T(8,128)(2,1)S(1)}, bf16[5,641,640]{2,1,0:T(8,128)(2,1)}, u32[]{:S(2)}) %copy-start) | copy-done | bytes 4102424
  3.5 0.0 copy-start.1
  3.5 1.1 %copy-done.1 = bf16[2,20,8,1280]{3,2,1,0:T(8,128)(2,1)S(1)} copy-done((bf16[2,20,8,1280]{3,2,1,0:T(8,128)(2,1)S(1)}, bf16[2,20,8,1280]{3,2,1,0:T(8,128)(2,1)}, u32[]{:S(2)}) %copy-start.1) | copy-done | bytes 819224
  4.6 0.0 copy-start.2
  4.6 0.7 %copy-done.2 = s32[320]{0:T(512)S(1)} copy-done((s32[320]{0:T(512)S(1)}, s32[320]{0:T(512)}, u32[]{:S(2)}) %copy-start.2) | copy-done | bytes 1304
  5.3 44.4 %shard_map.46 = bf16[2,10,8,1280]{3,2,1,0:T(8,128)(2,1)S(1)} custom-call(s32[320]{0:T(512)S(1)} %copy-done.2, s32[640,1]{1,0:T(8,128)S(1)} %reshape.8.wave_ref, bf16[2,20,8,1280]{3,2,1,0:T(8,128)(2,1)S(1)} %copy-done.1, bf16[5,641,1280]{2,1,0:T(8,128)(2,1)} %fwd_hbm.1, bf16[5,641,640]{2,1,0:T(8,128)(2,1)S(1)} %copy-done), custom_call_target="tpu_custom_call" | custom-call | tf_op jit(solution)/shard_map/pallas_call | solution.py:243
  49.7 0.8 %copy.12 = bf16[2,10,8,1280]{3,2,1,0:T(8,128)(2,1)} copy(bf16[2,10,8,1280]{3,2,1,0:T(8,128)(2,1)S(1)} %shard_map.46) | data formatting | bytes 819200
  (2 shorter events, 0.0 us)
Async XLA Ops:
  1.3 2.2 %copy-start = (bf16[5,641,640]{2,1,0:T(8,128)(2,1)S(1)}, bf16[5,641,640]{2,1,0:T(8,128)(2,1)}, u32[]{:S(2)}) copy-start(bf16[5,641,640]{2,1,0:T(8,128)(2,1)} %inv_hbm.1) | copy-start | bytes 12307204
  3.5 1.1 %copy-start.1 = (bf16[2,20,8,1280]{3,2,1,0:T(8,128)(2,1)S(1)}, bf16[2,20,8,1280]{3,2,1,0:T(8,128)(2,1)}, u32[]{:S(2)}) copy-start(bf16[2,20,8,1280]{3,2,1,0:T(8,128)(2,1)} %fine_ref.1) | copy-start | bytes 2457604
  4.6 0.7 %copy-start.2 = (s32[320]{0:T(512)S(1)}, s32[320]{0:T(512)}, u32[]{:S(2)}) copy-start(s32[320]{0:T(512)} %pair_ref.1) | copy-start | bytes 3844

commit v2 on v1

--- a/solution.py
+++ b/solution.py
@@ -13,6 +13,7 @@
 BAND = FINE // BANDS
 CBAND = COARSE // BANDS
 SLOTS = 5
+PAIRS = BANDS * SLOTS
 ROWS = 641
 BF = jnp.bfloat16
 F32 = jnp.float32
@@ -45,17 +46,38 @@
     )
 
 
+def peer(me, u):
+    ring = u // 8
+    step = 4 + ((ring + 1) // 2) * (2 * (ring % 2) - 1)
+    to = me + 16 * ((u % 8) // 2) + 2 * step + 1 - u % 2
+    return lax.rem(to, BANDS)
+
+
 def kernel(
-    pair_ref, wave_ref, fine_ref, fwd_hbm, inv_hbm, out_ref,
-    fwd, inv, folded, sel, wide, narrow, acc,
+    pair_hbm, fine_hbm, fwd_hbm, inv_hbm, out_ref,
+    pair_ref, line, column, fine_ref, fwd, inv, folded, sel, turned, wide, narrow, acc,
     send_ab, send_c, recv_ab, recv_c, back_ab, back_c, home_ab, home_c,
-    fwd_sem, inv_sem, out_sem1, in_sem1, out_sem2, in_sem2,
+    pair_sem, fine_sem, fwd_sem, inv_sem, out_sem1, in_sem1, out_sem2, in_sem2,
 ):
     me = lax.axis_index("lat")
     lev = lax.axis_index("lev")
     barrier = pltpu.get_barrier_semaphore()
 
-    @pl.loop(1, BANDS)
+    pieces = BAND // 4
+    pair_copies = [
+        pltpu.make_async_copy(pair_hbm, line, pair_sem.at[0]),
+        pltpu.make_async_copy(pair_hbm, pair_ref, pair_sem.at[1]),
+    ]
+    fine_copies = [
+        pltpu.make_async_copy(
+            fine_hbm.at[:, pl.ds(4 * q, 4)], fine_ref.at[:, pl.ds(4 * q, 4)], fine_sem.at[q]
+        )
+        for q in range(pieces)
+    ]
+    for copy in pair_copies + fine_copies:
+        copy.start()
+
+    @pl.loop(1, BANDS, unroll=True)
     def _(t):
         pl.semaphore_signal(
             barrier, inc=1, device_id=(lax.rem(me + t, BANDS), lev), device_id_type=MESH
@@ -65,8 +87,22 @@
         pltpu.make_async_copy(fwd_hbm.at[s], fwd.at[s], fwd_sem.at[s]).start()
         pltpu.make_async_copy(inv_hbm.at[s], inv.at[s], inv_sem.at[s]).start()
 
-    @pl.loop(0, BAND)
-    def _(i):
+    pair_copies[0].wait()
+    column[...] = jnp.transpose(jnp.broadcast_to(line[...].reshape(1, PAIRS), (128, PAIRS)))
+    for slot in range(SLOTS):
+        low = column[pl.ds(slot, BANDS, stride=SLOTS), :]
+        for k, wave in enumerate((low, WAVES - 1 - low)):
+            at = (2 * slot + k) * BANDS
+            for b in range(WAVES // 128):
+                sel[at : at + BANDS, 128 * b : 128 * (b + 1)] = jnp.where(
+                    wave == lanes(wave.shape) + 128 * b, 1.0, 0.0
+                ).astype(BF)
+
+    for at in (0, 256, 512):
+        count = min(256, WAVES - at)
+        turned[:, at : at + count] = jnp.transpose(sel[at : at + count, :])
+
+    def fold(i):
         north = fine_ref[0, i].astype(F32)
         south = fine_ref[1, i].astype(F32)
         m = lanes((8, 2 * WAVES))
@@ -77,22 +113,24 @@
         rows = jnp.concatenate(
             [even[:, :WAVES], even[:, WAVES:], odd[:, :WAVES], odd[:, WAVES:]], axis=0
         )
-        folded[pl.ds(pl.multiple_of(i * 32, 32), 32), :] = rows.astype(BF)
-
-    sel[...] = jnp.where(
-        wave_ref[...] == lanes((WAVES, WAVES)), 1.0, 0.0
-    ).astype(BF)
+        folded[32 * i : 32 * (i + 1), :] = rows.astype(BF)
+
+    def facing(a, b, high):
+        low = lanes(a.shape) < 64
+        if high:
+            return jnp.where(low, pltpu.roll(a, 64, 1), b)
+        return jnp.where(low, a, pltpu.roll(b, 64, 1))
 
     def pick(first, count):
-        return lax.dot_general(
-            sel[first : first + count, :], folded[...], (((1,), (1,)), ((), ())),
-            preferred_element_type=F32,
-        )
+        g = jnp.dot(
+            folded[...], turned[:, first : first + count], preferred_element_type=F32
+        )
+        return [g[32 * i : 32 * (i + 1)] for i in range(BAND)]
 
     def exchange(src, dst, out_sem, in_sem):
         pltpu.make_async_copy(src.at[me], dst.at[me], in_sem).start()
 
-        @pl.loop(1, BANDS)
+        @pl.loop(1, BANDS, unroll=9)
         def _(t):
             to = lax.rem(me + t, BANDS)
             pltpu.make_async_remote_copy(
@@ -107,27 +145,36 @@
         part = src.at[pl.ds(0, BANDS - 1)]
         pltpu.make_async_copy(part, part, out_sem).wait()
 
+    for q in range(pieces):
+        fine_copies[q].wait()
+        for i in range(4 * q, 4 * (q + 1)):
+            fold(i)
     for ch in range(2):
         g = pick(256 * ch, 256)
-        for q in range(BAND // 4):
-            cols = g[:, 128 * q : 128 * (q + 1)]
-            parts = block_transpose([cols[64 * k : 64 * (k + 1)] for k in range(4)])
+        for i in range(0, BAND, 2):
+            blocks = []
             for k in range(4):
-                wide[pl.ds(4 * q + k, BANDS, stride=BAND), :] = parts[k]
+                at = 128 * (k // 2)
+                a, b = g[i][:, at : at + 128], g[i + 1][:, at : at + 128]
+                blocks.append(facing(a, b, k % 2 == 1))
+            rows = jnp.transpose(jnp.concatenate(blocks, axis=0))
+            for k in range(2):
+                wide[pl.ds(i + k, BANDS, stride=BAND), :] = rows[64 * k : 64 * (k + 1)]
         send_ab.at[ch].reshape(FINE, 128)[...] = wide[...].astype(BF)
         if ch == 0:
             pl.semaphore_wait(barrier, BANDS - 1)
         exchange(send_ab.at[ch], recv_ab.at[ch], out_sem1.at[ch], in_sem1.at[ch])
 
     g = pick(512, 128)
-    for q in range(BAND // 4):
-        cols = g[:, 128 * q : 128 * (q + 1)]
-        parts = half_swap(cols[:64], cols[64:])
+    for i in range(0, BAND, 4):
+        blocks = [facing(g[i + k % 2], g[i + 2 + k % 2], k >= 2) for k in range(4)]
+        rows = jnp.transpose(jnp.concatenate(blocks, axis=0))
         for k in range(2):
-            wide[pl.ds(2 * q + k, BANDS, stride=BAND // 2), :] = parts[k]
+            wide[pl.ds(i // 2 + k, BANDS, stride=BAND // 2), :] = rows[64 * k : 64 * (k + 1)]
     send_c.reshape(FINE // 2, 128)[...] = wide[: FINE // 2].astype(BF)
     exchange(send_c, recv_c, out_sem1.at[2], in_sem1.at[2])
 
+    pair_copies[1].wait()
     row = lax.broadcasted_iota(jnp.int32, (ROWS, 128), 0)
     lane = lanes((ROWS, 128))
 
@@ -212,11 +259,9 @@
     for q in range(3):
         parts = half_swap(*[wide[pl.ds(2 * q + k, BANDS, stride=6), :] for k in range(2)])
         groups.append(jnp.concatenate(parts, axis=0).astype(BF))
-    acc[...] += place(512, jnp.concatenate(groups, axis=1))
-
-    @pl.loop(0, CBAND)
-    def _(j):
-        rows = acc[pl.ds(pl.multiple_of(j * 32, 32), 32), :]
+    placed = place(512, jnp.concatenate(groups, axis=1))
+    for j in range(CBAND):
+        rows = acc[32 * j : 32 * (j + 1), :] + placed[32 * j : 32 * (j + 1)]
         kept = 2 * lanes(rows.shape) < 20 + 4 * (me * CBAND + j)
         rows = jnp.where(kept, rows, 0.0).astype(BF)
         for h in range(2):
@@ -232,10 +277,8 @@
 
 
 def on_device(fine_field, fwd_table, inv_table, pair_order):
-    low = jnp.transpose(pair_order.reshape(BANDS, SLOTS))
-    waves = jnp.stack([low, WAVES - 1 - low], axis=1).reshape(WAVES, 1)
     vmem = pl.BlockSpec(memory_space=pltpu.VMEM)
-    hbm = pl.BlockSpec(memory_space=pl.ANY)
+    hbm = pl.BlockSpec(memory_space=pltpu.HBM)
     ab1 = (2, BANDS, BAND // 2, 2, 128)
     c1 = (BANDS, BAND // 4, 2, 128)
     ab2 = (2, BANDS, CBAND // 2, 2, 128)
@@ -243,12 +286,17 @@
     return pl.pallas_call(
         kernel,
         out_shape=jax.ShapeDtypeStruct((2, CBAND, 8, 2 * WAVES), BF),
-        in_specs=[pl.BlockSpec(memory_space=pltpu.SMEM), vmem, vmem, hbm, hbm],
+        in_specs=[hbm] * 4,
         out_specs=vmem,
         scratch_shapes=[
+            pltpu.SMEM((PAIRS,), jnp.int32),
+            pltpu.VMEM((PAIRS,), jnp.int32),
+            pltpu.VMEM((PAIRS, 128), jnp.int32),
+            pltpu.VMEM((2, BAND, 8, 2 * WAVES), BF),
             pltpu.VMEM((SLOTS, ROWS, FINE), BF),
             pltpu.VMEM((SLOTS, ROWS, COARSE), BF),
             pltpu.VMEM((BAND * 32, WAVES), BF),
+            pltpu.VMEM((WAVES, WAVES), BF),
             pltpu.VMEM((WAVES, WAVES), BF),
             pltpu.VMEM((FINE, 128), F32),
             pltpu.VMEM((6 * BANDS, 128), F32),
@@ -257,14 +305,15 @@
             pltpu.VMEM(ab1, BF), pltpu.VMEM(c1, BF),
             pltpu.VMEM(ab2, BF), pltpu.VMEM(c2, BF),
             pltpu.VMEM(ab2, BF), pltpu.VMEM(c2, BF),
+            pltpu.SemaphoreType.DMA((2,)), pltpu.SemaphoreType.DMA((BAND // 4,)),
             pltpu.SemaphoreType.DMA((SLOTS,)), pltpu.SemaphoreType.DMA((SLOTS,)),
             pltpu.SemaphoreType.DMA((3,)), pltpu.SemaphoreType.DMA((3,)),
             pltpu.SemaphoreType.DMA((3,)), pltpu.SemaphoreType.DMA((3,)),
         ],
         compiler_params=pltpu.CompilerParams(
-            collective_id=0, has_side_effects=True, vmem_limit_bytes=48 << 20
+            collective_id=0, has_side_effects=True, vmem_limit_bytes=55500000
         ),
-    )(pair_order, waves, fine_field, fwd_table, inv_table)
+    )(pair_order, fine_field, fwd_table, inv_table)
 
 
 def solution(mesh):

time: 50.7 us -> 45.1 us (0.89)
  local copies, waits for them, and re-layouts: 5.99 us -> 1.44 us
  Pallas kernels: 44.4 us -> 43.5 us
    unnamed x7 -> x3, local copies, waits for them, and re-layouts: 4.75 us -> 1.44 us
    reshape x2 -> x0, local copies, waits for them, and re-layouts: 1.08 us -> none  [the longest x1 0.81 us: on_device(): low = jnp.transpose(pair_order.reshape(BANDS, SLOTS))]
    pallas_call x1, Pallas kernels: 44.4 us -> 43.5 us  [on_device(): pl.pallas_call(kernel, out_shape=jax.ShapeDtypeStruct((2, CBAND, 8, 2 * W...]
where the time goes in v2:
time: 45.1 us; the launch traced here: 45 us
  Pallas kernels  43.5 us (96%)
  local copies, waits for them, and re-layouts  1.44 us (3%)
    pallas_call x1, Pallas kernels, on_device(): pl.pallas_call(kernel, out_shape=jax.ShapeDtypeStruct((2, CBAND, 8, 2 * W...  43.5 us
    unnamed x3, local copies, waits for them, and re-layouts  1.44 us

profile of v2, /device:TPU:1, one launch (start us, length us, event | category | flops | bytes accessed | tf_op | source)
XLA Modules:
  0.0 45.0 jit_solution(3811599008027623223)
XLA Ops:
  0.0 0.0 copy-start
  0.0 0.7 %copy-done = s32[320]{0:T(512)S(1)} copy-done((s32[320]{0:T(512)S(1)}, s32[320]{0:T(512)}, u32[]{:S(2)}) %copy-start) | copy-done | bytes 1304
  0.7 43.5 %shard_map.46 = bf16[2,10,8,1280]{3,2,1,0:T(8,128)(2,1)S(1)} custom-call(s32[320]{0:T(512)S(1)} %copy-done, bf16[2,20,8,1280]{3,2,1,0:T(8,128)(2,1)} %fine_hbm.1, bf16[5,641,1280]{2,1,0:T(8,128)(2,1)} %fwd_hbm.1, bf16[5,641,640]{2,1,0:T(8,128)(2,1)} %inv_hbm.1), custom_call_target="tpu_custom_call" | custom-call | tf_op jit(solution)/shard_map/pallas_call | solution.py:286
  44.2 0.8 %copy.6 = bf16[2,10,8,1280]{3,2,1,0:T(8,128)(2,1)} copy(bf16[2,10,8,1280]{3,2,1,0:T(8,128)(2,1)S(1)} %shard_map.46) | data formatting | bytes 819200
Async XLA Ops:
  0.0 0.7 %copy-start = (s32[320]{0:T(512)S(1)}, s32[320]{0:T(512)}, u32[]{:S(2)}) copy-start(s32[320]{0:T(512)} %pair_hbm.1) | copy-start | bytes 3844

commit v3 on v2

--- a/solution.py
+++ b/solution.py
@@ -15,6 +15,13 @@
 SLOTS = 5
 PAIRS = BANDS * SLOTS
 ROWS = 641
+ORDER = [
+    x * 16 + z * 2 + core
+    for core in (1, 0)
+    for x in (2, 1, 3, 0)
+    for z in (4, 3, 5, 2, 6, 1, 7, 0)
+    if (x, z, core) != (0, 0, 0)
+]
 BF = jnp.bfloat16
 F32 = jnp.float32
 
@@ -46,13 +53,6 @@
     )
 
 
-def peer(me, u):
-    ring = u // 8
-    step = 4 + ((ring + 1) // 2) * (2 * (ring % 2) - 1)
-    to = me + 16 * ((u % 8) // 2) + 2 * step + 1 - u % 2
-    return lax.rem(to, BANDS)
-
-
 def kernel(
     pair_hbm, fine_hbm, fwd_hbm, inv_hbm, out_ref,
     pair_ref, line, column, fine_ref, fwd, inv, folded, sel, turned, wide, narrow, acc,
@@ -83,9 +83,6 @@
             barrier, inc=1, device_id=(lax.rem(me + t, BANDS), lev), device_id_type=MESH
         )
 
-    for s in range(SLOTS):
-        pltpu.make_async_copy(fwd_hbm.at[s], fwd.at[s], fwd_sem.at[s]).start()
-        pltpu.make_async_copy(inv_hbm.at[s], inv.at[s], inv_sem.at[s]).start()
 
     pair_copies[0].wait()
     column[...] = jnp.transpose(jnp.broadcast_to(line[...].reshape(1, PAIRS), (128, PAIRS)))
@@ -130,8 +127,7 @@
     def exchange(src, dst, out_sem, in_sem):
         pltpu.make_async_copy(src.at[me], dst.at[me], in_sem).start()
 
-        @pl.loop(1, BANDS, unroll=9)
-        def _(t):
+        for t in ORDER:
             to = lax.rem(me + t, BANDS)
             pltpu.make_async_remote_copy(
                 src_ref=src.at[to], dst_ref=dst.at[me], send_sem=out_sem, recv_sem=in_sem,
@@ -173,6 +169,9 @@
             wide[pl.ds(i // 2 + k, BANDS, stride=BAND // 2), :] = rows[64 * k : 64 * (k + 1)]
     send_c.reshape(FINE // 2, 128)[...] = wide[: FINE // 2].astype(BF)
     exchange(send_c, recv_c, out_sem1.at[2], in_sem1.at[2])
+    for s in range(SLOTS):
+        pltpu.make_async_copy(fwd_hbm.at[s], fwd.at[s], fwd_sem.at[s]).start()
+        pltpu.make_async_copy(inv_hbm.at[s], inv.at[s], inv_sem.at[s]).start()
 
     pair_copies[1].wait()
     row = lax.broadcasted_iota(jnp.int32, (ROWS, 128), 0)
@@ -248,7 +247,7 @@
                     block_transpose([wide[pl.ds(j, BANDS, stride=CBAND), :] for j in js]), axis=0
                 ).astype(BF)
             )
-        placed = place(256 * ch, jnp.concatenate(groups, axis=1))
+        placed = place(256 * ch, jnp.concatenate(groups, axis=1)[:, :320])
         if ch == 0:
             acc[...] = placed
         else:
@@ -259,7 +258,7 @@
     for q in range(3):
         parts = half_swap(*[wide[pl.ds(2 * q + k, BANDS, stride=6), :] for k in range(2)])
         groups.append(jnp.concatenate(parts, axis=0).astype(BF))
-    placed = place(512, jnp.concatenate(groups, axis=1))
+    placed = place(512, jnp.concatenate(groups, axis=1)[:, :320])
     for j in range(CBAND):
         rows = acc[32 * j : 32 * (j + 1), :] + placed[32 * j : 32 * (j + 1)]
         kept = 2 * lanes(rows.shape) < 20 + 4 * (me * CBAND + j)
@@ -300,7 +299,7 @@
             pltpu.VMEM((WAVES, WAVES), BF),
             pltpu.VMEM((FINE, 128), F32),
             pltpu.VMEM((6 * BANDS, 128), F32),
-            pltpu.VMEM((384, WAVES), F32),
+            pltpu.VMEM((320, WAVES), F32),
             pltpu.VMEM(ab1, BF), pltpu.VMEM(c1, BF),
             pltpu.VMEM(ab1, BF), pltpu.VMEM(c1, BF),
             pltpu.VMEM(ab2, BF), pltpu.VMEM(c2, BF),

time: 45.1 us -> 43.6 us (0.967)
  Pallas kernels: 43.5 us -> 42 us
    pallas_call x1, Pallas kernels: 43.5 us -> 42 us  [on_device(): pl.pallas_call(kernel, out_shape=jax.ShapeDtypeStruct((2, CBAND, 8, 2 * W...]
where the time goes in v3:
time: 43.6 us; the launch traced here: 43.5 us
  Pallas kernels  42 us (96%)
  local copies, waits for them, and re-layouts  1.44 us (3%)
    pallas_call x1, Pallas kernels, on_device(): pl.pallas_call(kernel, out_shape=jax.ShapeDtypeStruct((2, CBAND, 8, 2 * W...  42 us
    unnamed x3, local copies, waits for them, and re-layouts  1.44 us

profile of v3, /device:TPU:1, one launch (start us, length us, event | category | flops | bytes accessed | tf_op | source)
XLA Modules:
  0.0 43.5 jit_solution(12941116495334113009)
XLA Ops:
  0.0 0.0 copy-start
  0.0 0.7 %copy-done = s32[320]{0:T(512)S(1)} copy-done((s32[320]{0:T(512)S(1)}, s32[320]{0:T(512)}, u32[]{:S(2)}) %copy-start) | copy-done | bytes 1304
  0.7 42.0 %shard_map.46 = bf16[2,10,8,1280]{3,2,1,0:T(8,128)(2,1)S(1)} custom-call(s32[320]{0:T(512)S(1)} %copy-done, bf16[2,20,8,1280]{3,2,1,0:T(8,128)(2,1)} %fine_hbm.1, bf16[5,641,1280]{2,1,0:T(8,128)(2,1)} %fwd_hbm.1, bf16[5,641,640]{2,1,0:T(8,128)(2,1)} %inv_hbm.1), custom_call_target="tpu_custom_call" | custom-call | tf_op jit(solution)/shard_map/pallas_call | solution.py:285
  42.7 0.8 %copy.6 = bf16[2,10,8,1280]{3,2,1,0:T(8,128)(2,1)} copy(bf16[2,10,8,1280]{3,2,1,0:T(8,128)(2,1)S(1)} %shard_map.46) | data formatting | bytes 819200
Async XLA Ops:
  0.0 0.7 %copy-start = (s32[320]{0:T(512)S(1)}, s32[320]{0:T(512)}, u32[]{:S(2)}) copy-start(s32[320]{0:T(512)} %pair_hbm.1) | copy-start | bytes 3844

commit v4 on v3

--- a/solution.py
+++ b/solution.py
@@ -77,8 +77,7 @@
     for copy in pair_copies + fine_copies:
         copy.start()
 
-    @pl.loop(1, BANDS, unroll=True)
-    def _(t):
+    for t in ORDER:
         pl.semaphore_signal(
             barrier, inc=1, device_id=(lax.rem(me + t, BANDS), lev), device_id_type=MESH
         )

time: 43.6 us -> 43.3 us (level)
  no operation moved by 1% of the time
where the time goes in v4:
time: 43.3 us; the launch traced here: 43.2 us
  Pallas kernels  41.8 us (97%)
  local copies, waits for them, and re-layouts  1.44 us (3%)
    pallas_call x1, Pallas kernels, on_device(): pl.pallas_call(kernel, out_shape=jax.ShapeDtypeStruct((2, CBAND, 8, 2 * W...  41.8 us
    unnamed x3, local copies, waits for them, and re-layouts  1.44 us

profile of v4, /device:TPU:1, one launch (start us, length us, event | category | flops | bytes accessed | tf_op | source)
XLA Modules:
  0.0 43.2 jit_solution(13857351468685397034)
XLA Ops:
  0.0 0.0 copy-start
  0.0 0.7 %copy-done = s32[320]{0:T(512)S(1)} copy-done((s32[320]{0:T(512)S(1)}, s32[320]{0:T(512)}, u32[]{:S(2)}) %copy-start) | copy-done | bytes 1304
  0.7 41.8 %shard_map.46 = bf16[2,10,8,1280]{3,2,1,0:T(8,128)(2,1)S(1)} custom-call(s32[320]{0:T(512)S(1)} %copy-done, bf16[2,20,8,1280]{3,2,1,0:T(8,128)(2,1)} %fine_hbm.1, bf16[5,641,1280]{2,1,0:T(8,128)(2,1)} %fwd_hbm.1, bf16[5,641,640]{2,1,0:T(8,128)(2,1)} %inv_hbm.1), custom_call_target="tpu_custom_call" | custom-call | tf_op jit(solution)/shard_map/pallas_call | solution.py:284
  42.5 0.8 %copy.6 = bf16[2,10,8,1280]{3,2,1,0:T(8,128)(2,1)} copy(bf16[2,10,8,1280]{3,2,1,0:T(8,128)(2,1)S(1)} %shard_map.46) | data formatting | bytes 819200
Async XLA Ops:
  0.0 0.7 %copy-start = (s32[320]{0:T(512)S(1)}, s32[320]{0:T(512)}, u32[]{:S(2)}) copy-start(s32[320]{0:T(512)} %pair_hbm.1) | copy-start | bytes 3844
